TPU v7x, 32 devices: a whole 2x2x4 slice. The times are simulated.
32 devices in a mesh: ta: 2 (over y), gz: 4 (over x, core), xy: 4 (over z).
Axes of the slice: x: 2, y: 2, z: 4, core: 2. Of those that a mesh axis runs over, the one named last changes fastest.
Arguments:
- right_side: float32 [2, 4, 4, 2, 32, 128], P('ta', 'gz', 'xy'), may hold values from -40 to 40
- stencil: float32 [2, 4, 4, 2, 9, 128, 128], P('ta', 'gz', 'xy'), may hold values from -0.5 to 1.5, as said below
- restrict: float32 [2, 4, 4, 2, 32, 128], P('ta', 'gz', 'xy'), may hold values from -0.5 to 0.5
- aggregate: int32 [2, 4, 4, 2], P('ta', 'gz', 'xy'), may hold values from 0 to 3, as said below
- coarsest_inverse: float32 [128, 128], P('xy'), may hold values from -0.5 to 0.5
Outputs:
- solution: float32 [2, 4, 4, 2, 32, 128], P('ta', 'gz', 'xy')
- residual: float32 [2, 4, 4, 2, 32, 128], P('ta', 'gz', 'xy')
Inputs may be any that keep to these rules, and one draw needn't show every extreme that they name: `aggregate`: sites are grouped into 2 x 2 x 2 x 2 blocks aligned at even coordinates; each block forms one coarsest site, and the coarsest sites are numbered in an order drawn from the seed. `stencil`: each self block is close to the identity; the other blocks are small and full.
All inputs are finite; a program needn't handle non-finite values.
Results may differ from a plain program's by a relative error of at most 0.0001.
Values sent between devices are 32-bit elements; how exact they have to be, the bound alone decides.
A program may use at most 64 MiB of HBM per device.

v0:
```python
import functools
import itertools

import jax
import jax.numpy as jnp
from jax import lax
from jax.experimental import pallas as pl
from jax.experimental.pallas import tpu as pltpu
from jax.sharding import PartitionSpec as P

AXES = ("ta", "gz", "xy")
F32 = jnp.float32
BF16 = jnp.bfloat16
MESH = pl.DeviceIdType.MESH


def split(x):
    high = x.astype(BF16)
    return high, (x - high.astype(F32)).astype(BF16)


def dot_nt(a, b):
    return lax.dot_general(a, b, (((1,), (1,)), ((), ())), preferred_element_type=F32)


def dot_nn(a, b):
    return lax.dot_general(a, b, (((1,), (0,)), ((), ())), preferred_element_type=F32)


def stack_split(x):
    return jnp.concatenate(split(x), axis=0)


def fold(o):
    r, n = o.shape[0] // 2, o.shape[1] // 2
    return o[:r, :n] + (o[:r, n:] + o[r:, :n])


def loop(n, step, init, most=8):
    if n <= most:
        for i in range(n):
            init = step(i, init)
        return init
    return lax.fori_loop(0, n, step, init)


def kernel(
    sizes, agg_in, b_in, sten_in, res_in, inv_in, sol_ref, resid_ref,
    agg_ref, b_ref, res_ref, in_sem, sten, sw, rp, halo1, halo2, w1, w2, inv, lab, wr, near_e, far_e, near_l, far_l,
    sten_sem, h1s, h1r, h2s, h2r, ivs, ivr, lbs, lbr, nes, ner, fes, fer, nls, nlr, fls, flr,
):
    xs, nrhs, comps = b_ref.shape
    k3 = res_ref.shape[1]
    na, _, nc3 = inv.shape
    per = inv_in.shape[0]
    groups = far_e.shape[0]
    packs = comps // k3
    part = nrhs // packs
    width = xs * comps
    me = tuple(lax.axis_index(a) for a in AXES)

    def at(offset):
        return {a: lax.rem(i + o, n) for a, i, o, n in zip(AXES, me, offset, sizes)}

    def across(bits):
        return {a: (i + 1 - 2 * lax.rem(i, 2)) if f else i for a, i, f in zip(AXES, me, bits)}

    def line(axis, o):
        return tuple(o if a == axis else 0 for a in range(3))

    halo_sends = []
    for a in (2, 1, 0):
        halo_sends.append((2 * a, line(a, sizes[a] - 1)))
        if sizes[a] > 2:
            halo_sends.append((2 * a + 1, line(a, 1)))
    near_sends = [bits for bits in itertools.product((0, 1), repeat=3) if any(bits)]
    far_sends = [
        tuple(2 * o for o in offs)
        for offs in itertools.product(*(range(n // 2) for n in sizes))
        if any(offs)
    ]
    inv_sends = [line(2, o) for o in range(1, sizes[2])]

    barrier = pltpu.get_barrier_semaphore()
    offsets = sorted({o for _, o in halo_sends} | set(far_sends) | set(inv_sends))
    diagonals = [bits for bits in near_sends if sum(bits) > 1]
    for device in [at(o) for o in offsets] + [across(f) for f in diagonals]:
        pl.semaphore_signal(barrier, inc=1, device_id=device, device_id_type=MESH)

    mine = inv.at[pl.ds(me[2] * per, per)]
    loads = [
        pltpu.make_async_copy(src, dst, in_sem.at[i])
        for i, (src, dst) in enumerate(
            ((b_in, b_ref), (agg_in, agg_ref), (res_in, res_ref), (inv_in, mine))
        )
    ]
    copies = [
        pltpu.make_async_copy(sten_in.at[x], sten.at[x], sten_sem.at[x]) for x in range(xs)
    ]
    for c in loads + copies:
        c.start()

    pl.semaphore_wait(barrier, len(offsets) + len(diagonals))

    def remote(src, dst, send, recv, device):
        return pltpu.make_async_remote_copy(
            src_ref=src, dst_ref=dst, send_sem=send, recv_sem=recv,
            device_id=device, device_id_type=MESH,
        )

    def start_halo(src, halo, send, recv):
        out = [remote(src, halo.at[s], send.at[s], recv.at[s], at(o)) for s, o in halo_sends]
        for c in out:
            c.start()
        return out

    first = start_halo(b_in, halo1, h1s, h1r)

    for c in loads:
        c.wait()
    lab[0] = jnp.full(lab.shape[1:], agg_ref[0].astype(F32), F32)
    for x in range(xs):
        high, low = split(jnp.concatenate([res_ref[x]] * packs, axis=0))
        rp[pl.ds(0, comps), pl.ds(x * comps, comps)] = high
        rp[pl.ds(comps, comps), pl.ds(x * comps, comps)] = low
    early = [
        remote(mine, mine, ivs.at[i], ivr.at[i], at(o))
        for i, o in enumerate(inv_sends)
    ] + [
        remote(lab.at[0], lab.at[i + 1], lbs.at[i], lbr.at[i], at(o))
        for i, o in enumerate(far_sends)
    ]
    for c in early:
        c.start()

    inside = ((0,), (7, 8)) if xs == 2 else ((0,), (7,), (8,))
    sides, slots = [(), ()], [(), ()]
    for a in range(3):
        pair = ((1 + 2 * a,), (2 + 2 * a,))
        sides[a // 2] += pair if sizes[a] > 2 else (pair[0] + pair[1],)
        slots[a // 2] += (2 * a, 2 * a + 1) if sizes[a] > 2 else (2 * a,)

    for x in range(xs):
        copies[x].wait()
        for i, ks in enumerate(inside + sides[0] + sides[1]):
            high, low = split(sum(sten[x, k] for k in ks))
            cols = pl.ds(i * comps, comps)
            sw[x, pl.ds(0, comps), cols] = high
            sw[x, pl.ds(comps, comps), cols] = low

    def multiply(x, fields, begin):
        lhs = stack_split(jnp.concatenate(fields, axis=1))
        return dot_nt(lhs, sw[x, :, pl.ds(begin * comps, len(fields) * comps)])

    def local_part(field):
        out = []
        for x in range(xs):
            fields = [field[x], field[(x + 1) % xs]]
            if xs > 2:
                fields.append(field[(x + xs - 1) % xs])
            out.append(multiply(x, fields, 0))
        return out

    def halo_part(halo, base, sends):
        for group in range(2):
            for (slot, _), c in zip(halo_sends, sends):
                if slot in slots[group]:
                    c.wait_recv()
            begin = len(inside) + (len(sides[0]) if group else 0)
            base = [
                base[x] + multiply(x, [halo[i, x] for i in slots[group]], begin)
                for x in range(xs)
            ]
        return [fold(o) for o in base]

    lane = lax.broadcasted_iota(jnp.int32, (part, comps), 1)
    slot = lane // k3
    place = lax.rem(lane, k3)

    def pack(full):
        out = full[:part]
        for q in range(1, packs):
            out = jnp.where(slot == q, full[q * part : (q + 1) * part], out)
        return out

    def restricted(field):
        return pack(fold(dot_nt(stack_split(jnp.concatenate(field, axis=1)), rp[...])))

    def product(u, v, i):
        total = sum(u[x] * v[x] for x in range(xs))
        total = jnp.sum(total, axis=1, keepdims=True)
        return jnp.where(place == i, pack(jnp.broadcast_to(total, (nrhs, comps))), 0.0)

    def to_near(near, send, recv):
        out = [
            remote(near.at[0], near.at[i + 1], send.at[i], recv.at[i], across(f))
            for i, f in enumerate(near_sends)
        ]
        for c in out:
            c.start()
        return out

    def to_far(near, far, send, recv):
        total = near[0]
        for i in range(len(near_sends)):
            total = total + near[i + 1]
        far[0] = total
        out = [
            remote(far.at[0], far.at[i + 1], send.at[i], recv.at[i], at(o))
            for i, o in enumerate(far_sends)
        ]
        for c in out:
            c.start()
        return out

    bs = [b_ref[x] for x in range(xs)]
    base = local_part(bs)
    near_e[0, pl.ds(0, part)] = restricted(bs)
    w1s = halo_part(halo1, base, first)
    for x in range(xs):
        w1[x] = w1s[x]
    second = start_halo(w1, halo2, h2s, h2r)

    near_e[0, pl.ds(part, part)] = restricted(w1s)
    near_e[0, pl.ds(2 * part, part)] = product(w1s, w1s, 0) + product(w1s, bs, 1)
    third_e = to_near(near_e, nes, ner)
    base = local_part(w1s)
    for c in early:
        c.wait_recv()

    own = inv[agg_ref[0]]
    own_high, own_low = split(own)
    rows = lax.broadcasted_iota(jnp.int32, (comps, nc3), 0)
    cols = lax.broadcasted_iota(jnp.int32, (comps, nc3), 1)
    same = lax.rem(rows, k3) == lax.rem(cols, k3)
    block = (cols // k3).astype(F32)
    vec_high, vec_low = split(jnp.concatenate([res_ref[x] for x in range(xs)], axis=1))

    def prepare(g, carry):
        label = lab[g][0:1, 0:1]
        pick = jnp.where(same & (block == label), 1.0, 0.0).astype(BF16)
        weights = dot_nt(pick, own_high) + dot_nt(pick, own_low)
        high, low = split(weights)
        lift = dot_nn(high, vec_high) + (dot_nn(high, vec_low) + dot_nn(low, vec_high))
        high, low = split(lift)
        first_row = g * comps if isinstance(g, int) else pl.multiple_of(g * comps, comps)
        wr[pl.ds(first_row, comps), pl.ds(0, width)] = high
        wr[pl.ds(first_row, comps), pl.ds(width, width)] = low
        return carry

    loop(groups, prepare, 0)

    w2s = halo_part(halo2, base, second)
    near_l[0, pl.ds(0, part)] = restricted(w2s)
    near_l[0, pl.ds(part, part)] = (
        product(w1s, w2s, 2) + product(w2s, w2s, 3) + product(w2s, bs, 4)
    )
    third_l = to_near(near_l, nls, nlr)
    for x in range(xs):
        w2[x] = w2s[x]
    for c in third_e:
        c.wait_recv()
    fourth_e = to_far(near_e, far_e, fes, fer)
    for c in third_l:
        c.wait_recv()
    fourth_l = to_far(near_l, far_l, fls, flr)
    for c in first + early + second + third_e + third_l:
        c.wait_send()
    for c in fourth_e + fourth_l:
        c.wait_recv()

    def add(g, acc):
        return acc + (far_e[g, pl.ds(2 * part, part)] + far_l[g, pl.ds(part, part)])

    square = loop(groups, add, jnp.zeros((part, comps), F32))
    cross, corr, square2, cross2 = (pltpu.roll(square, comps - i, 1) for i in range(1, 5))
    step = cross / square
    ratio = corr / square
    turn = (step * corr - cross2) / (square2 - ratio * corr)
    push = step + turn * ratio

    def spread(coef):
        return jnp.concatenate(
            [
                jnp.broadcast_to(coef[:, q * k3 : q * k3 + 1], (part, comps))
                for q in range(packs)
            ],
            axis=0,
        )

    push, turn = spread(push), spread(turn)
    push_packed, turn_packed = pack(push), pack(turn)

    def coarse(g):
        mixed = (
            far_e[g, pl.ds(0, part)]
            - push_packed * far_e[g, pl.ds(part, part)]
            + turn_packed * far_l[g, pl.ds(0, part)]
        )
        return jnp.concatenate([jnp.where(slot == q, mixed, 0.0) for q in range(packs)], axis=0)

    pair = 2 if groups % 2 == 0 else 1

    def lift_step(h, acc):
        lhs = jnp.concatenate([coarse(h * pair + j) for j in range(pair)], axis=1)
        rows = pair * comps
        first_row = h * rows if isinstance(h, int) else pl.multiple_of(h * rows, rows)
        return acc + dot_nn(stack_split(lhs), wr[pl.ds(first_row, rows), :])

    lifted = fold(loop(groups // pair, lift_step, jnp.zeros((2 * nrhs, 2 * width), F32)))
    for x in range(xs):
        bx, ux, vx = b_ref[x], w1[x], w2[x]
        resid_ref[x] = bx - push * ux + turn * vx
        sol_ref[x] = (push * bx - turn * ux) + lifted[:, x * comps : (x + 1) * comps]
    for c in fourth_e + fourth_l:
        c.wait_send()


def finish(sol_ref, resid_ref, sol_out, resid_out, sem):
    out = [
        pltpu.make_async_copy(src, dst, sem.at[i])
        for i, (src, dst) in enumerate(((sol_ref, sol_out), (resid_ref, resid_out)))
    ]
    for c in out:
        c.start()
    for c in out:
        c.wait()


def body(sizes, right_side, stencil, restrict, aggregate, coarsest_inverse):
    shape = right_side.shape
    xs, nrhs, comps = shape[3:]
    k3 = restrict.shape[4]
    nc3 = coarsest_inverse.shape[1]
    na = nc3 // k3
    groups = (sizes[0] // 2) * (sizes[1] // 2) * (sizes[2] // 2)
    per = coarsest_inverse.shape[0] // k3
    part = nrhs * k3 // comps
    blocks = 9 - (xs == 2) - sum(n == 2 for n in sizes)
    vmem = pl.BlockSpec(memory_space=pltpu.VMEM)
    dma = pltpu.SemaphoreType.DMA
    field = jax.ShapeDtypeStruct((xs, nrhs, comps), F32)
    sol, resid = pl.pallas_call(
        functools.partial(kernel, sizes),
        out_shape=(field, field),
        in_specs=[pl.BlockSpec(memory_space=pltpu.HBM)] * 5,
        out_specs=(vmem, vmem),
        scratch_shapes=[
            pltpu.SMEM((xs,), jnp.int32),
            pltpu.VMEM((xs, nrhs, comps), F32),
            pltpu.VMEM((xs, k3, comps), F32),
            dma((4,)),
            pltpu.VMEM((xs, 9, comps, comps), F32),
            pltpu.VMEM((xs, 2 * comps, blocks * comps), BF16),
            pltpu.VMEM((2 * comps, xs * comps), BF16),
            pltpu.VMEM((6, xs, nrhs, comps), F32),
            pltpu.VMEM((6, xs, nrhs, comps), F32),
            pltpu.VMEM((xs, nrhs, comps), F32),
            pltpu.VMEM((xs, nrhs, comps), F32),
            pltpu.VMEM((na, k3, nc3), F32),
            pltpu.VMEM((groups, 8, comps), F32),
            pltpu.VMEM((groups * comps, 2 * xs * comps), BF16),
            pltpu.VMEM((8, 3 * part, comps), F32),
            pltpu.VMEM((groups, 3 * part, comps), F32),
            pltpu.VMEM((8, 2 * part, comps), F32),
            pltpu.VMEM((groups, 2 * part, comps), F32),
            dma((xs,)),
            dma((6,)), dma((6,)), dma((6,)), dma((6,)),
            dma((sizes[2],)), dma((sizes[2],)),
            dma((groups,)), dma((groups,)),
            dma((7,)), dma((7,)), dma((groups,)), dma((groups,)),
            dma((7,)), dma((7,)), dma((groups,)), dma((groups,)),
        ],
        compiler_params=pltpu.CompilerParams(
            collective_id=0,
            has_side_effects=True,
            vmem_limit_bytes=(16 if groups <= 8 else 48) * 2**20,
        ),
    )(
        *(
            pltpu.with_memory_space_constraint(a, pltpu.HBM)
            for a in (
                aggregate.reshape(xs),
                right_side.reshape(xs, nrhs, comps),
                stencil.reshape(xs, 9, comps, comps),
                restrict.reshape(xs, k3, comps),
                coarsest_inverse.reshape(per, k3, nc3),
            )
        )
    )
    sol, resid = pl.pallas_call(
        finish,
        out_shape=(field, field),
        in_specs=[vmem, vmem],
        out_specs=[pl.BlockSpec(memory_space=pl.ANY)] * 2,
        scratch_shapes=[dma((2,))],
        compiler_params=pltpu.CompilerParams(vmem_limit_bytes=2**20),
    )(sol, resid)
    return sol.reshape(shape), resid.reshape(shape)


def solution(mesh):
    sizes = tuple(mesh.shape[a] for a in AXES)
    return jax.shard_map(
        functools.partial(body, sizes),
        mesh=mesh,
        in_specs=(
            P("ta", "gz", "xy", None, None, None),
            P("ta", "gz", "xy", None, None, None, None),
            P("ta", "gz", "xy", None, None, None),
            P("ta", "gz", "xy", None),
            P("xy", None),
        ),
        out_specs=(P("ta", "gz", "xy", None, None, None), P("ta", "gz", "xy", None, None, None)),
        check_vma=False,
    )
```

profile of v0, /device:TPU:0, one launch (start us, length us, event | category | flops | bytes accessed | tf_op | source)
XLA Modules:
  0.0 23.6 jit_solution(15817608634521556098)
XLA Ops:
  0.6 22.3 %shard_map.68 = (f32[2,32,128]{2,1,0:T(8,128)S(1)}, f32[2,32,128]{2,1,0:T(8,128)S(1)}) custom-call(s32[2]{0:T(128)} %bitcast.11, f32[2,32,128]{2,1,0:T(8,128)} %bitcast.8, f32[2,9,128,128]{3,2,1,0:T(8,128)} %bitcast.7, f32[2,32,128]{2,1,0:T(8,128)} %bitcast.9, f32[1,32,128]{2,1,0:T(8,128)} %bitcast.10), custom_call_target="tpu_custom_call" | custom-call | tf_op jit(solution)/shard_map/pallas_call | solution.py:343
  23.0 0.6 %shard_map.69 = (f32[2,32,128]{2,1,0:T(8,128)}, f32[2,32,128]{2,1,0:T(8,128)}) custom-call(f32[2,32,128]{2,1,0:T(8,128)S(1)} %get-tuple-element.6.sol_ref, f32[2,32,128]{2,1,0:T(8,128)S(1)} %get-tuple-element.7.resid_ref), custom_call_target="tpu_custom_call" | custom-call | tf_op jit(solution)/shard_map/pallas_call | solution.py:391
where the time goes:
time: 23.8 us; the launch traced here: 23.6 us
  Pallas kernels  23 us (97%)
  between operations  0.64 us (3%)
    pallas_call x1, Pallas kernels, body(): pl.pallas_call(functools.partial(kernel, sizes), out_shape=(field, field)...  22.3 us
    pallas_call x1, Pallas kernels, body(): pl.pallas_call(finish, out_shape=(field, field), in_specs=[vmem, vmem], o...  0.65 us

commit v1 on v0

--- a/solution.py
+++ b/solution.py
@@ -124,14 +124,14 @@
         rp[pl.ds(0, comps), pl.ds(x * comps, comps)] = high
         rp[pl.ds(comps, comps), pl.ds(x * comps, comps)] = low
     early = [
-        remote(mine, mine, ivs.at[i], ivr.at[i], at(o))
-        for i, o in enumerate(inv_sends)
-    ] + [
         remote(lab.at[0], lab.at[i + 1], lbs.at[i], lbr.at[i], at(o))
         for i, o in enumerate(far_sends)
     ]
     for c in early:
         c.start()
+    gather = [
+        remote(mine, mine, ivs.at[i], ivr.at[i], at(o)) for i, o in enumerate(inv_sends)
+    ]
 
     inside = ((0,), (7, 8)) if xs == 2 else ((0,), (7,), (8,))
     sides, slots = [(), ()], [(), ()]
@@ -161,11 +161,14 @@
             out.append(multiply(x, fields, 0))
         return out
 
-    def halo_part(halo, base, sends):
+    def halo_part(halo, base, sends, then=()):
         for group in range(2):
             for (slot, _), c in zip(halo_sends, sends):
                 if slot in slots[group]:
                     c.wait_recv()
+            if group:
+                for c in then:
+                    c.start()
             begin = len(inside) + (len(sides[0]) if group else 0)
             base = [
                 base[x] + multiply(x, [halo[i, x] for i in slots[group]], begin)
@@ -216,7 +219,7 @@
     bs = [b_ref[x] for x in range(xs)]
     base = local_part(bs)
     near_e[0, pl.ds(0, part)] = restricted(bs)
-    w1s = halo_part(halo1, base, first)
+    w1s = halo_part(halo1, base, first, gather)
     for x in range(xs):
         w1[x] = w1s[x]
     second = start_halo(w1, halo2, h2s, h2r)
@@ -225,31 +228,6 @@
     near_e[0, pl.ds(2 * part, part)] = product(w1s, w1s, 0) + product(w1s, bs, 1)
     third_e = to_near(near_e, nes, ner)
     base = local_part(w1s)
-    for c in early:
-        c.wait_recv()
-
-    own = inv[agg_ref[0]]
-    own_high, own_low = split(own)
-    rows = lax.broadcasted_iota(jnp.int32, (comps, nc3), 0)
-    cols = lax.broadcasted_iota(jnp.int32, (comps, nc3), 1)
-    same = lax.rem(rows, k3) == lax.rem(cols, k3)
-    block = (cols // k3).astype(F32)
-    vec_high, vec_low = split(jnp.concatenate([res_ref[x] for x in range(xs)], axis=1))
-
-    def prepare(g, carry):
-        label = lab[g][0:1, 0:1]
-        pick = jnp.where(same & (block == label), 1.0, 0.0).astype(BF16)
-        weights = dot_nt(pick, own_high) + dot_nt(pick, own_low)
-        high, low = split(weights)
-        lift = dot_nn(high, vec_high) + (dot_nn(high, vec_low) + dot_nn(low, vec_high))
-        high, low = split(lift)
-        first_row = g * comps if isinstance(g, int) else pl.multiple_of(g * comps, comps)
-        wr[pl.ds(first_row, comps), pl.ds(0, width)] = high
-        wr[pl.ds(first_row, comps), pl.ds(width, width)] = low
-        return carry
-
-    loop(groups, prepare, 0)
-
     w2s = halo_part(halo2, base, second)
     near_l[0, pl.ds(0, part)] = restricted(w2s)
     near_l[0, pl.ds(part, part)] = (
@@ -264,7 +242,32 @@
     for c in third_l:
         c.wait_recv()
     fourth_l = to_far(near_l, far_l, fls, flr)
-    for c in first + early + second + third_e + third_l:
+    for c in early + gather:
+        c.wait_recv()
+
+    own = inv[agg_ref[0]]
+    own_high, own_low = split(own)
+    rows = lax.broadcasted_iota(jnp.int32, (comps, nc3), 0)
+    cols = lax.broadcasted_iota(jnp.int32, (comps, nc3), 1)
+    same = lax.rem(rows, k3) == lax.rem(cols, k3)
+    block = (cols // k3).astype(F32)
+    vec_high, vec_low = split(jnp.concatenate([res_ref[x] for x in range(xs)], axis=1))
+
+    def prepare(g, carry):
+        label = lab[g][0:1, 0:1]
+        pick = jnp.where(same & (block == label), 1.0, 0.0).astype(BF16)
+        weights = dot_nt(pick, own_high) + dot_nt(pick, own_low)
+        high, low = split(weights)
+        lift = dot_nn(high, vec_high) + (dot_nn(high, vec_low) + dot_nn(low, vec_high))
+        high, low = split(lift)
+        first_row = g * comps if isinstance(g, int) else pl.multiple_of(g * comps, comps)
+        wr[pl.ds(first_row, comps), pl.ds(0, width)] = high
+        wr[pl.ds(first_row, comps), pl.ds(width, width)] = low
+        return carry
+
+    loop(groups, prepare, 0)
+
+    for c in first + early + gather + second + third_e + third_l:
         c.wait_send()
     for c in fourth_e + fourth_l:
         c.wait_recv()

time: 23.8 us -> 24.5 us (1.029)
  Pallas kernels: 23 us -> 23.7 us
    pallas_call x1, Pallas kernels: 22.3 us -> 23 us  [body(): pl.pallas_call(functools.partial(kernel, sizes), out_shape=(field, field)...]
where the time goes in v1:
time: 24.5 us; the launch traced here: 24.3 us
  Pallas kernels  23.7 us (97%)
  between operations  0.64 us (3%)
    pallas_call x1, Pallas kernels, body(): pl.pallas_call(functools.partial(kernel, sizes), out_shape=(field, field)...  23 us
    pallas_call x1, Pallas kernels, body(): pl.pallas_call(finish, out_shape=(field, field), in_specs=[vmem, vmem], o...  0.65 us

profile of v1, /device:TPU:0, one launch (start us, length us, event | category | flops | bytes accessed | tf_op | source)
XLA Modules:
  0.0 24.3 jit_solution(7637753009548286599)
XLA Ops:
  0.6 23.0 %shard_map.68 = (f32[2,32,128]{2,1,0:T(8,128)S(1)}, f32[2,32,128]{2,1,0:T(8,128)S(1)}) custom-call(s32[2]{0:T(128)} %bitcast.11, f32[2,32,128]{2,1,0:T(8,128)} %bitcast.8, f32[2,9,128,128]{3,2,1,0:T(8,128)} %bitcast.7, f32[2,32,128]{2,1,0:T(8,128)} %bitcast.9, f32[1,32,128]{2,1,0:T(8,128)} %bitcast.10), custom_call_target="tpu_custom_call" | custom-call | tf_op jit(solution)/shard_map/pallas_call | solution.py:346
  23.7 0.6 %shard_map.69 = (f32[2,32,128]{2,1,0:T(8,128)}, f32[2,32,128]{2,1,0:T(8,128)}) custom-call(f32[2,32,128]{2,1,0:T(8,128)S(1)} %get-tuple-element.6.sol_ref, f32[2,32,128]{2,1,0:T(8,128)S(1)} %get-tuple-element.7.resid_ref), custom_call_target="tpu_custom_call" | custom-call | tf_op jit(solution)/shard_map/pallas_call | solution.py:394

commit v2 on v0

--- a/solution.py
+++ b/solution.py
@@ -46,14 +46,14 @@
 
 def kernel(
     sizes, agg_in, b_in, sten_in, res_in, inv_in, sol_ref, resid_ref,
-    agg_ref, b_ref, res_ref, in_sem, sten, sw, rp, halo1, halo2, w1, w2, inv, lab, wr, near_e, far_e, near_l, far_l,
-    sten_sem, h1s, h1r, h2s, h2r, ivs, ivr, lbs, lbr, nes, ner, fes, fer, nls, nlr, fls, flr,
+    agg_ref, b_ref, res_ref, in_sem, sten, sw, rp, halo1, halo2, w1, w2, inv, lab, wr, near, far,
+    sten_sem, h1s, h1r, h2s, h2r, ivs, ivr, lbs, lbr, nrs, nrr, frs, frr,
 ):
     xs, nrhs, comps = b_ref.shape
     k3 = res_ref.shape[1]
     na, _, nc3 = inv.shape
     per = inv_in.shape[0]
-    groups = far_e.shape[0]
+    groups = far.shape[1]
     packs = comps // k3
     part = nrhs // packs
     width = xs * comps
@@ -74,6 +74,7 @@
         if sizes[a] > 2:
             halo_sends.append((2 * a + 1, line(a, 1)))
     near_sends = [bits for bits in itertools.product((0, 1), repeat=3) if any(bits)]
+    near_sends.sort(key=lambda f: -(f[0] + f[2]))
     far_sends = [
         tuple(2 * o for o in offs)
         for offs in itertools.product(*(range(n // 2) for n in sizes))
@@ -175,7 +176,6 @@
 
     lane = lax.broadcasted_iota(jnp.int32, (part, comps), 1)
     slot = lane // k3
-    place = lax.rem(lane, k3)
 
     def pack(full):
         out = full[:part]
@@ -186,28 +186,38 @@
     def restricted(field):
         return pack(fold(dot_nt(stack_split(jnp.concatenate(field, axis=1)), rp[...])))
 
-    def product(u, v, i):
-        total = sum(u[x] * v[x] for x in range(xs))
-        total = jnp.sum(total, axis=1, keepdims=True)
-        return jnp.where(place == i, pack(jnp.broadcast_to(total, (nrhs, comps))), 0.0)
-
-    def to_near(near, send, recv):
+    ones = jnp.ones((16, comps), BF16)
+
+    def products(*pairs):
+        rows = [sum(u[x] * v[x] for x in range(xs)) for u, v in pairs]
+        if len(rows) < packs:
+            rows.append(jnp.zeros(((packs - len(rows)) * nrhs, comps), F32))
+        high, low = split(jnp.concatenate(rows, axis=0))
+        return (dot_nt(ones, high) + dot_nt(ones, low))[:1]
+
+    def to_near(i, count):
+        here = pl.ds(0, count)
         out = [
-            remote(near.at[0], near.at[i + 1], send.at[i], recv.at[i], across(f))
-            for i, f in enumerate(near_sends)
+            remote(
+                near.at[i, 0, here], near.at[i, j + 1, here], nrs.at[i, j], nrr.at[i, j], across(f)
+            )
+            for j, f in enumerate(near_sends)
         ]
         for c in out:
             c.start()
         return out
 
-    def to_far(near, far, send, recv):
-        total = near[0]
-        for i in range(len(near_sends)):
-            total = total + near[i + 1]
-        far[0] = total
+    def to_far(i, count, arriving):
+        here = pl.ds(0, count)
+        for c in arriving:
+            c.wait_recv()
+        total = near[i, 0, here]
+        for j in range(len(near_sends)):
+            total = total + near[i, j + 1, here]
+        far[i, 0, here] = total
         out = [
-            remote(far.at[0], far.at[i + 1], send.at[i], recv.at[i], at(o))
-            for i, o in enumerate(far_sends)
+            remote(far.at[i, 0, here], far.at[i, j + 1, here], frs.at[i, j], frr.at[i, j], at(o))
+            for j, o in enumerate(far_sends)
         ]
         for c in out:
             c.start()
@@ -215,15 +225,17 @@
 
     bs = [b_ref[x] for x in range(xs)]
     base = local_part(bs)
-    near_e[0, pl.ds(0, part)] = restricted(bs)
+    near[0, 0, pl.ds(0, part)] = restricted(bs)
+    near_b = to_near(0, part)
     w1s = halo_part(halo1, base, first)
     for x in range(xs):
         w1[x] = w1s[x]
     second = start_halo(w1, halo2, h2s, h2r)
 
-    near_e[0, pl.ds(part, part)] = restricted(w1s)
-    near_e[0, pl.ds(2 * part, part)] = product(w1s, w1s, 0) + product(w1s, bs, 1)
-    third_e = to_near(near_e, nes, ner)
+    near[1, 0, pl.ds(0, part)] = restricted(w1s)
+    near[1, 0, pl.ds(part, 1)] = products((w1s, w1s), (w1s, bs))
+    near_1 = to_near(1, part + 1)
+    far_b = to_far(0, part, near_b)
     base = local_part(w1s)
     for c in early:
         c.wait_recv()
@@ -251,51 +263,47 @@
     loop(groups, prepare, 0)
 
     w2s = halo_part(halo2, base, second)
-    near_l[0, pl.ds(0, part)] = restricted(w2s)
-    near_l[0, pl.ds(part, part)] = (
-        product(w1s, w2s, 2) + product(w2s, w2s, 3) + product(w2s, bs, 4)
-    )
-    third_l = to_near(near_l, nls, nlr)
+    near[2, 0, pl.ds(0, part)] = restricted(w2s)
+    near[2, 0, pl.ds(part, 1)] = products((w1s, w2s), (w2s, w2s), (w2s, bs))
+    near_2 = to_near(2, part + 1)
     for x in range(xs):
         w2[x] = w2s[x]
-    for c in third_e:
+    far_1 = to_far(1, part + 1, near_1)
+    far_2 = to_far(2, part + 1, near_2)
+    for c in first + early + second + near_b + near_1 + near_2:
+        c.wait_send()
+    for c in far_b + far_1 + far_2:
         c.wait_recv()
-    fourth_e = to_far(near_e, far_e, fes, fer)
-    for c in third_l:
-        c.wait_recv()
-    fourth_l = to_far(near_l, far_l, fls, flr)
-    for c in first + early + second + third_e + third_l:
-        c.wait_send()
-    for c in fourth_e + fourth_l:
-        c.wait_recv()
 
     def add(g, acc):
-        return acc + (far_e[g, pl.ds(2 * part, part)] + far_l[g, pl.ds(part, part)])
-
-    square = loop(groups, add, jnp.zeros((part, comps), F32))
-    cross, corr, square2, cross2 = (pltpu.roll(square, comps - i, 1) for i in range(1, 5))
+        return acc[0] + far[1, g, pl.ds(part, 1)], acc[1] + far[2, g, pl.ds(part, 1)]
+
+    blank = jnp.zeros((1, comps), F32)
+    square, corr = loop(groups, add, (blank, blank))
+    cross = pltpu.roll(square, comps - nrhs, 1)
+    square2 = pltpu.roll(corr, comps - nrhs, 1)
+    cross2 = pltpu.roll(corr, comps - 2 * nrhs, 1)
     step = cross / square
     ratio = corr / square
     turn = (step * corr - cross2) / (square2 - ratio * corr)
     push = step + turn * ratio
 
+    own_lane = lax.broadcasted_iota(jnp.int32, (nrhs, comps), 0) == lax.broadcasted_iota(
+        jnp.int32, (nrhs, comps), 1
+    )
+
     def spread(coef):
-        return jnp.concatenate(
-            [
-                jnp.broadcast_to(coef[:, q * k3 : q * k3 + 1], (part, comps))
-                for q in range(packs)
-            ],
-            axis=0,
-        )
+        column = jnp.where(own_lane, jnp.broadcast_to(coef, (nrhs, comps)), 0.0)
+        return jnp.broadcast_to(jnp.sum(column, axis=1, keepdims=True), (nrhs, comps))
 
     push, turn = spread(push), spread(turn)
     push_packed, turn_packed = pack(push), pack(turn)
 
     def coarse(g):
         mixed = (
-            far_e[g, pl.ds(0, part)]
-            - push_packed * far_e[g, pl.ds(part, part)]
-            + turn_packed * far_l[g, pl.ds(0, part)]
+            far[0, g, pl.ds(0, part)]
+            - push_packed * far[1, g, pl.ds(0, part)]
+            + turn_packed * far[2, g, pl.ds(0, part)]
         )
         return jnp.concatenate([jnp.where(slot == q, mixed, 0.0) for q in range(packs)], axis=0)
 
@@ -312,7 +320,7 @@
         bx, ux, vx = b_ref[x], w1[x], w2[x]
         resid_ref[x] = bx - push * ux + turn * vx
         sol_ref[x] = (push * bx - turn * ux) + lifted[:, x * comps : (x + 1) * comps]
-    for c in fourth_e + fourth_l:
+    for c in far_b + far_1 + far_2:
         c.wait_send()
 
 
@@ -360,16 +368,13 @@
             pltpu.VMEM((na, k3, nc3), F32),
             pltpu.VMEM((groups, 8, comps), F32),
             pltpu.VMEM((groups * comps, 2 * xs * comps), BF16),
-            pltpu.VMEM((8, 3 * part, comps), F32),
-            pltpu.VMEM((groups, 3 * part, comps), F32),
-            pltpu.VMEM((8, 2 * part, comps), F32),
-            pltpu.VMEM((groups, 2 * part, comps), F32),
+            pltpu.VMEM((3, 8, 2 * part, comps), F32),
+            pltpu.VMEM((3, groups, 2 * part, comps), F32),
             dma((xs,)),
             dma((6,)), dma((6,)), dma((6,)), dma((6,)),
             dma((sizes[2],)), dma((sizes[2],)),
             dma((groups,)), dma((groups,)),
-            dma((7,)), dma((7,)), dma((groups,)), dma((groups,)),
-            dma((7,)), dma((7,)), dma((groups,)), dma((groups,)),
+            dma((3, 7)), dma((3, 7)), dma((3, groups)), dma((3, groups)),
         ],
         compiler_params=pltpu.CompilerParams(
             collective_id=0,

time: 23.8 us -> 23.8 us (level)
  no operation moved by 1% of the time
where the time goes in v2:
time: 23.8 us; the launch traced here: 23.6 us
  Pallas kernels  23 us (97%)
  between operations  0.64 us (3%)
    pallas_call x1, Pallas kernels, body(): pl.pallas_call(functools.partial(kernel, sizes), out_shape=(field, field)...  22.4 us
    pallas_call x1, Pallas kernels, body(): pl.pallas_call(finish, out_shape=(field, field), in_specs=[vmem, vmem], o...  0.65 us

profile of v2, /device:TPU:0, one launch (start us, length us, event | category | flops | bytes accessed | tf_op | source)
XLA Modules:
  0.0 23.6 jit_solution(577562084208009670)
XLA Ops:
  0.6 22.4 %shard_map.68 = (f32[2,32,128]{2,1,0:T(8,128)S(1)}, f32[2,32,128]{2,1,0:T(8,128)S(1)}) custom-call(s32[2]{0:T(128)} %bitcast.11, f32[2,32,128]{2,1,0:T(8,128)} %bitcast.8, f32[2,9,128,128]{3,2,1,0:T(8,128)} %bitcast.7, f32[2,32,128]{2,1,0:T(8,128)} %bitcast.9, f32[1,32,128]{2,1,0:T(8,128)} %bitcast.10), custom_call_target="tpu_custom_call" | custom-call | tf_op jit(solution)/shard_map/pallas_call | solution.py:351
  23.0 0.6 %shard_map.69 = (f32[2,32,128]{2,1,0:T(8,128)}, f32[2,32,128]{2,1,0:T(8,128)}) custom-call(f32[2,32,128]{2,1,0:T(8,128)S(1)} %get-tuple-element.6.sol_ref, f32[2,32,128]{2,1,0:T(8,128)S(1)} %get-tuple-element.7.resid_ref), custom_call_target="tpu_custom_call" | custom-call | tf_op jit(solution)/shard_map/pallas_call | solution.py:396

commit v3 on v2

--- a/solution.py
+++ b/solution.py
@@ -85,6 +85,7 @@
     barrier = pltpu.get_barrier_semaphore()
     offsets = sorted({o for _, o in halo_sends} | set(far_sends) | set(inv_sends))
     diagonals = [bits for bits in near_sends if sum(bits) > 1]
+    offsets.sort(key=lambda o: o not in [h for _, h in halo_sends])
     for device in [at(o) for o in offsets] + [across(f) for f in diagonals]:
         pl.semaphore_signal(barrier, inc=1, device_id=device, device_id_type=MESH)
 
@@ -226,17 +227,23 @@
     bs = [b_ref[x] for x in range(xs)]
     base = local_part(bs)
     near[0, 0, pl.ds(0, part)] = restricted(bs)
-    near_b = to_near(0, part)
     w1s = halo_part(halo1, base, first)
     for x in range(xs):
         w1[x] = w1s[x]
     second = start_halo(w1, halo2, h2s, h2r)
 
-    near[1, 0, pl.ds(0, part)] = restricted(w1s)
-    near[1, 0, pl.ds(part, 1)] = products((w1s, w1s), (w1s, bs))
-    near_1 = to_near(1, part + 1)
-    far_b = to_far(0, part, near_b)
     base = local_part(w1s)
+    near[0, 0, pl.ds(part, part)] = restricted(w1s)
+    near[0, 0, pl.ds(2 * part, 1)] = products((w1s, w1s), (w1s, bs))
+    near_e = to_near(0, 2 * part + 1)
+    w2s = halo_part(halo2, base, second)
+    near[1, 0, pl.ds(0, part)] = restricted(w2s)
+    near[1, 0, pl.ds(part, 1)] = products((w1s, w2s), (w2s, w2s), (w2s, bs))
+    near_l = to_near(1, part + 1)
+    for x in range(xs):
+        w2[x] = w2s[x]
+    far_e = to_far(0, 2 * part + 1, near_e)
+
     for c in early:
         c.wait_recv()
 
@@ -262,21 +269,45 @@
 
     loop(groups, prepare, 0)
 
-    w2s = halo_part(halo2, base, second)
-    near[2, 0, pl.ds(0, part)] = restricted(w2s)
-    near[2, 0, pl.ds(part, 1)] = products((w1s, w2s), (w2s, w2s), (w2s, bs))
-    near_2 = to_near(2, part + 1)
-    for x in range(xs):
-        w2[x] = w2s[x]
-    far_1 = to_far(1, part + 1, near_1)
-    far_2 = to_far(2, part + 1, near_2)
-    for c in first + early + second + near_b + near_1 + near_2:
+    pair = 2 if groups % 2 == 0 else 1
+
+    def unpack(packed):
+        return jnp.concatenate([jnp.where(slot == q, packed, 0.0) for q in range(packs)], axis=0)
+
+    def lift(i, count):
+        def lift_step(h, acc):
+            lhs = jnp.concatenate(
+                [
+                    jnp.concatenate(
+                        [
+                            unpack(far[i, h * pair + j, pl.ds(f * part, part)])
+                            for f in range(count)
+                        ],
+                        axis=0,
+                    )
+                    for j in range(pair)
+                ],
+                axis=1,
+            )
+            rows = pair * comps
+            first_row = h * rows if isinstance(h, int) else pl.multiple_of(h * rows, rows)
+            return acc + dot_nn(stack_split(lhs), wr[pl.ds(first_row, rows), :])
+
+        zero = jnp.zeros((2 * count * nrhs, 2 * width), F32)
+        return fold(loop(groups // pair, lift_step, zero))
+
+    far_l = to_far(1, part + 1, near_l)
+    for c in first + early + second + near_e + near_l:
         c.wait_send()
-    for c in far_b + far_1 + far_2:
+    for c in far_e:
         c.wait_recv()
+    lift_early = lift(0, 2)
+    for c in far_l:
+        c.wait_recv()
+    lift_late = lift(1, 1)
 
     def add(g, acc):
-        return acc[0] + far[1, g, pl.ds(part, 1)], acc[1] + far[2, g, pl.ds(part, 1)]
+        return acc[0] + far[0, g, pl.ds(2 * part, 1)], acc[1] + far[1, g, pl.ds(part, 1)]
 
     blank = jnp.zeros((1, comps), F32)
     square, corr = loop(groups, add, (blank, blank))
@@ -297,30 +328,17 @@
         return jnp.broadcast_to(jnp.sum(column, axis=1, keepdims=True), (nrhs, comps))
 
     push, turn = spread(push), spread(turn)
-    push_packed, turn_packed = pack(push), pack(turn)
-
-    def coarse(g):
-        mixed = (
-            far[0, g, pl.ds(0, part)]
-            - push_packed * far[1, g, pl.ds(0, part)]
-            + turn_packed * far[2, g, pl.ds(0, part)]
-        )
-        return jnp.concatenate([jnp.where(slot == q, mixed, 0.0) for q in range(packs)], axis=0)
-
-    pair = 2 if groups % 2 == 0 else 1
-
-    def lift_step(h, acc):
-        lhs = jnp.concatenate([coarse(h * pair + j) for j in range(pair)], axis=1)
-        rows = pair * comps
-        first_row = h * rows if isinstance(h, int) else pl.multiple_of(h * rows, rows)
-        return acc + dot_nn(stack_split(lhs), wr[pl.ds(first_row, rows), :])
-
-    lifted = fold(loop(groups // pair, lift_step, jnp.zeros((2 * nrhs, 2 * width), F32)))
     for x in range(xs):
+        cols = slice(x * comps, (x + 1) * comps)
         bx, ux, vx = b_ref[x], w1[x], w2[x]
         resid_ref[x] = bx - push * ux + turn * vx
-        sol_ref[x] = (push * bx - turn * ux) + lifted[:, x * comps : (x + 1) * comps]
-    for c in far_b + far_1 + far_2:
+        sol_ref[x] = (
+            (push * bx - turn * ux)
+            + lift_early[:nrhs, cols]
+            - push * lift_early[nrhs:, cols]
+            + turn * lift_late[:, cols]
+        )
+    for c in far_e + far_l:
         c.wait_send()
 
 
@@ -368,13 +386,13 @@
             pltpu.VMEM((na, k3, nc3), F32),
             pltpu.VMEM((groups, 8, comps), F32),
             pltpu.VMEM((groups * comps, 2 * xs * comps), BF16),
-            pltpu.VMEM((3, 8, 2 * part, comps), F32),
-            pltpu.VMEM((3, groups, 2 * part, comps), F32),
+            pltpu.VMEM((2, 8, 3 * part, comps), F32),
+            pltpu.VMEM((2, groups, 3 * part, comps), F32),
             dma((xs,)),
             dma((6,)), dma((6,)), dma((6,)), dma((6,)),
             dma((sizes[2],)), dma((sizes[2],)),
             dma((groups,)), dma((groups,)),
-            dma((3, 7)), dma((3, 7)), dma((3, groups)), dma((3, groups)),
+            dma((2, 7)), dma((2, 7)), dma((2, groups)), dma((2, groups)),
         ],
         compiler_params=pltpu.CompilerParams(
             collective_id=0,

time: 23.8 us -> 23.5 us (0.987)
  Pallas kernels: 23 us -> 22.7 us
    pallas_call x1, Pallas kernels: 22.4 us -> 22.1 us  [body(): pl.pallas_call(functools.partial(kernel, sizes), out_shape=(field, field)...]
where the time goes in v3:
time: 23.5 us; the launch traced here: 23.3 us
  Pallas kernels  22.7 us (97%)
  between operations  0.64 us (3%)
    pallas_call x1, Pallas kernels, body(): pl.pallas_call(functools.partial(kernel, sizes), out_shape=(field, field)...  22.1 us
    pallas_call x1, Pallas kernels, body(): pl.pallas_call(finish, out_shape=(field, field), in_specs=[vmem, vmem], o...  0.65 us

profile of v3, /device:TPU:0, one launch (start us, length us, event | category | flops | bytes accessed | tf_op | source)
XLA Modules:
  0.0 23.3 jit_solution(1603014476233131186)
XLA Ops:
  0.6 22.1 %shard_map.68 = (f32[2,32,128]{2,1,0:T(8,128)S(1)}, f32[2,32,128]{2,1,0:T(8,128)S(1)}) custom-call(s32[2]{0:T(128)} %bitcast.11, f32[2,32,128]{2,1,0:T(8,128)} %bitcast.8, f32[2,9,128,128]{3,2,1,0:T(8,128)} %bitcast.7, f32[2,32,128]{2,1,0:T(8,128)} %bitcast.9, f32[1,32,128]{2,1,0:T(8,128)} %bitcast.10), custom_call_target="tpu_custom_call" | custom-call | tf_op jit(solution)/shard_map/pallas_call | solution.py:369
  22.7 0.6 %shard_map.69 = (f32[2,32,128]{2,1,0:T(8,128)}, f32[2,32,128]{2,1,0:T(8,128)}) custom-call(f32[2,32,128]{2,1,0:T(8,128)S(1)} %get-tuple-element.6.sol_ref, f32[2,32,128]{2,1,0:T(8,128)S(1)} %get-tuple-element.7.resid_ref), custom_call_target="tpu_custom_call" | custom-call | tf_op jit(solution)/shard_map/pallas_call | solution.py:414

commit v4 on v3

--- a/solution.py
+++ b/solution.py
@@ -122,9 +122,9 @@
         c.wait()
     lab[0] = jnp.full(lab.shape[1:], agg_ref[0].astype(F32), F32)
     for x in range(xs):
-        high, low = split(jnp.concatenate([res_ref[x]] * packs, axis=0))
-        rp[pl.ds(0, comps), pl.ds(x * comps, comps)] = high
-        rp[pl.ds(comps, comps), pl.ds(x * comps, comps)] = low
+        high, low = split(jnp.transpose(jnp.concatenate([res_ref[x]] * packs, axis=0)))
+        rp[pl.ds(x * comps, comps), pl.ds(0, comps)] = high
+        rp[pl.ds(x * comps, comps), pl.ds(comps, comps)] = low
     early = [
         remote(mine, mine, ivs.at[i], ivr.at[i], at(o))
         for i, o in enumerate(inv_sends)
@@ -145,14 +145,14 @@
     for x in range(xs):
         copies[x].wait()
         for i, ks in enumerate(inside + sides[0] + sides[1]):
-            high, low = split(sum(sten[x, k] for k in ks))
-            cols = pl.ds(i * comps, comps)
-            sw[x, pl.ds(0, comps), cols] = high
-            sw[x, pl.ds(comps, comps), cols] = low
+            high, low = split(jnp.transpose(sum(sten[x, k] for k in ks)))
+            rows = pl.ds(i * comps, comps)
+            sw[x, rows, pl.ds(0, comps)] = high
+            sw[x, rows, pl.ds(comps, comps)] = low
 
     def multiply(x, fields, begin):
         lhs = stack_split(jnp.concatenate(fields, axis=1))
-        return dot_nt(lhs, sw[x, :, pl.ds(begin * comps, len(fields) * comps)])
+        return dot_nn(lhs, sw[x, pl.ds(begin * comps, len(fields) * comps), :])
 
     def local_part(field):
         out = []
@@ -185,16 +185,13 @@
         return out
 
     def restricted(field):
-        return pack(fold(dot_nt(stack_split(jnp.concatenate(field, axis=1)), rp[...])))
-
-    ones = jnp.ones((16, comps), BF16)
+        return pack(fold(dot_nn(stack_split(jnp.concatenate(field, axis=1)), rp[...])))
 
     def products(*pairs):
         rows = [sum(u[x] * v[x] for x in range(xs)) for u, v in pairs]
         if len(rows) < packs:
             rows.append(jnp.zeros(((packs - len(rows)) * nrhs, comps), F32))
-        high, low = split(jnp.concatenate(rows, axis=0))
-        return (dot_nt(ones, high) + dot_nt(ones, low))[:1]
+        return jnp.sum(jnp.transpose(jnp.concatenate(rows, axis=0)), axis=0, keepdims=True)
 
     def to_near(i, count):
         here = pl.ds(0, count)
@@ -377,8 +374,8 @@
             pltpu.VMEM((xs, k3, comps), F32),
             dma((4,)),
             pltpu.VMEM((xs, 9, comps, comps), F32),
-            pltpu.VMEM((xs, 2 * comps, blocks * comps), BF16),
-            pltpu.VMEM((2 * comps, xs * comps), BF16),
+            pltpu.VMEM((xs, blocks * comps, 2 * comps), BF16),
+            pltpu.VMEM((xs * comps, 2 * comps), BF16),
             pltpu.VMEM((6, xs, nrhs, comps), F32),
             pltpu.VMEM((6, xs, nrhs, comps), F32),
             pltpu.VMEM((xs, nrhs, comps), F32),

time: 23.5 us -> 23.4 us (level)
  no operation moved by 1% of the time
where the time goes in v4:
time: 23.4 us; the launch traced here: 23.2 us
  Pallas kernels  22.6 us (97%)
  between operations  0.64 us (3%)
    pallas_call x1, Pallas kernels, body(): pl.pallas_call(functools.partial(kernel, sizes), out_shape=(field, field)...  21.9 us
    pallas_call x1, Pallas kernels, body(): pl.pallas_call(finish, out_shape=(field, field), in_specs=[vmem, vmem], o...  0.65 us

profile of v4, /device:TPU:0, one launch (start us, length us, event | category | flops | bytes accessed | tf_op | source)
XLA Modules:
  0.0 23.2 jit_solution(17378500171141178628)
XLA Ops:
  0.6 21.9 %shard_map.68 = (f32[2,32,128]{2,1,0:T(8,128)S(1)}, f32[2,32,128]{2,1,0:T(8,128)S(1)}) custom-call(s32[2]{0:T(128)} %bitcast.11, f32[2,32,128]{2,1,0:T(8,128)} %bitcast.8, f32[2,9,128,128]{3,2,1,0:T(8,128)} %bitcast.7, f32[2,32,128]{2,1,0:T(8,128)} %bitcast.9, f32[1,32,128]{2,1,0:T(8,128)} %bitcast.10), custom_call_target="tpu_custom_call" | custom-call | tf_op jit(solution)/shard_map/pallas_call | solution.py:366
  22.6 0.6 %shard_map.69 = (f32[2,32,128]{2,1,0:T(8,128)}, f32[2,32,128]{2,1,0:T(8,128)}) custom-call(f32[2,32,128]{2,1,0:T(8,128)S(1)} %get-tuple-element.6.sol_ref, f32[2,32,128]{2,1,0:T(8,128)S(1)} %get-tuple-element.7.resid_ref), custom_call_target="tpu_custom_call" | custom-call | tf_op jit(solution)/shard_map/pallas_call | solution.py:411

commit v5 on v4

--- a/solution.py
+++ b/solution.py
@@ -126,9 +126,6 @@
         rp[pl.ds(x * comps, comps), pl.ds(0, comps)] = high
         rp[pl.ds(x * comps, comps), pl.ds(comps, comps)] = low
     early = [
-        remote(mine, mine, ivs.at[i], ivr.at[i], at(o))
-        for i, o in enumerate(inv_sends)
-    ] + [
         remote(lab.at[0], lab.at[i + 1], lbs.at[i], lbr.at[i], at(o))
         for i, o in enumerate(far_sends)
     ]
@@ -237,34 +234,14 @@
     near[1, 0, pl.ds(0, part)] = restricted(w2s)
     near[1, 0, pl.ds(part, 1)] = products((w1s, w2s), (w2s, w2s), (w2s, bs))
     near_l = to_near(1, part + 1)
+    gather = [
+        remote(mine, mine, ivs.at[i], ivr.at[i], at(o)) for i, o in enumerate(inv_sends)
+    ]
+    for c in gather:
+        c.start()
     for x in range(xs):
         w2[x] = w2s[x]
     far_e = to_far(0, 2 * part + 1, near_e)
-
-    for c in early:
-        c.wait_recv()
-
-    own = inv[agg_ref[0]]
-    own_high, own_low = split(own)
-    rows = lax.broadcasted_iota(jnp.int32, (comps, nc3), 0)
-    cols = lax.broadcasted_iota(jnp.int32, (comps, nc3), 1)
-    same = lax.rem(rows, k3) == lax.rem(cols, k3)
-    block = (cols // k3).astype(F32)
-    vec_high, vec_low = split(jnp.concatenate([res_ref[x] for x in range(xs)], axis=1))
-
-    def prepare(g, carry):
-        label = lab[g][0:1, 0:1]
-        pick = jnp.where(same & (block == label), 1.0, 0.0).astype(BF16)
-        weights = dot_nt(pick, own_high) + dot_nt(pick, own_low)
-        high, low = split(weights)
-        lift = dot_nn(high, vec_high) + (dot_nn(high, vec_low) + dot_nn(low, vec_high))
-        high, low = split(lift)
-        first_row = g * comps if isinstance(g, int) else pl.multiple_of(g * comps, comps)
-        wr[pl.ds(first_row, comps), pl.ds(0, width)] = high
-        wr[pl.ds(first_row, comps), pl.ds(width, width)] = low
-        return carry
-
-    loop(groups, prepare, 0)
 
     pair = 2 if groups % 2 == 0 else 1
 
@@ -294,7 +271,32 @@
         return fold(loop(groups // pair, lift_step, zero))
 
     far_l = to_far(1, part + 1, near_l)
-    for c in first + early + second + near_e + near_l:
+    for c in early + gather:
+        c.wait_recv()
+
+    own = inv[agg_ref[0]]
+    own_high, own_low = split(own)
+    rows = lax.broadcasted_iota(jnp.int32, (comps, nc3), 0)
+    cols = lax.broadcasted_iota(jnp.int32, (comps, nc3), 1)
+    same = lax.rem(rows, k3) == lax.rem(cols, k3)
+    block = (cols // k3).astype(F32)
+    vec_high, vec_low = split(jnp.concatenate([res_ref[x] for x in range(xs)], axis=1))
+
+    def prepare(g, carry):
+        label = lab[g][0:1, 0:1]
+        pick = jnp.where(same & (block == label), 1.0, 0.0).astype(BF16)
+        weights = dot_nt(pick, own_high) + dot_nt(pick, own_low)
+        high, low = split(weights)
+        lift = dot_nn(high, vec_high) + (dot_nn(high, vec_low) + dot_nn(low, vec_high))
+        high, low = split(lift)
+        first_row = g * comps if isinstance(g, int) else pl.multiple_of(g * comps, comps)
+        wr[pl.ds(first_row, comps), pl.ds(0, width)] = high
+        wr[pl.ds(first_row, comps), pl.ds(width, width)] = low
+        return carry
+
+    loop(groups, prepare, 0)
+
+    for c in first + early + gather + second + near_e + near_l:
         c.wait_send()
     for c in far_e:
         c.wait_recv()

time: 23.4 us -> 23 us (0.983)
  Pallas kernels: 22.6 us -> 22.2 us
    pallas_call x1, Pallas kernels: 21.9 us -> 21.5 us  [body(): pl.pallas_call(functools.partial(kernel, sizes), out_shape=(field, field)...]
where the time goes in v5:
time: 23 us; the launch traced here: 22.8 us
  Pallas kernels  22.2 us (97%)
  between operations  0.64 us (3%)
    pallas_call x1, Pallas kernels, body(): pl.pallas_call(functools.partial(kernel, sizes), out_shape=(field, field)...  21.5 us
    pallas_call x1, Pallas kernels, body(): pl.pallas_call(finish, out_shape=(field, field), in_specs=[vmem, vmem], o...  0.65 us

profile of v5, /device:TPU:0, one launch (start us, length us, event | category | flops | bytes accessed | tf_op | source)
XLA Modules:
  0.0 22.8 jit_solution(16241919662308721044)
XLA Ops:
  0.6 21.5 %shard_map.68 = (f32[2,32,128]{2,1,0:T(8,128)S(1)}, f32[2,32,128]{2,1,0:T(8,128)S(1)}) custom-call(s32[2]{0:T(128)} %bitcast.11, f32[2,32,128]{2,1,0:T(8,128)} %bitcast.8, f32[2,9,128,128]{3,2,1,0:T(8,128)} %bitcast.7, f32[2,32,128]{2,1,0:T(8,128)} %bitcast.9, f32[1,32,128]{2,1,0:T(8,128)} %bitcast.10), custom_call_target="tpu_custom_call" | custom-call | tf_op jit(solution)/shard_map/pallas_call | solution.py:368
  22.2 0.6 %shard_map.69 = (f32[2,32,128]{2,1,0:T(8,128)}, f32[2,32,128]{2,1,0:T(8,128)}) custom-call(f32[2,32,128]{2,1,0:T(8,128)S(1)} %get-tuple-element.6.sol_ref, f32[2,32,128]{2,1,0:T(8,128)S(1)} %get-tuple-element.7.resid_ref), custom_call_target="tpu_custom_call" | custom-call | tf_op jit(solution)/shard_map/pallas_call | solution.py:413

commit v6 on v5

--- a/solution.py
+++ b/solution.py
@@ -68,11 +68,12 @@
     def line(axis, o):
         return tuple(o if a == axis else 0 for a in range(3))
 
-    halo_sends = []
-    for a in (2, 1, 0):
-        halo_sends.append((2 * a, line(a, sizes[a] - 1)))
-        if sizes[a] > 2:
-            halo_sends.append((2 * a + 1, line(a, 1)))
+    halo_sends, slots = [], [(), ()]
+    for a in range(3):
+        for o in (sizes[a] - 1, 1)[: 2 if sizes[a] > 2 else 1]:
+            slots[a // 2] += (len(halo_sends),)
+            halo_sends.append((len(halo_sends), line(a, o)))
+    halo_sends.reverse()
     near_sends = [bits for bits in itertools.product((0, 1), repeat=3) if any(bits)]
     near_sends.sort(key=lambda f: -(f[0] + f[2]))
     far_sends = [
@@ -110,13 +111,15 @@
             device_id=device, device_id_type=MESH,
         )
 
+    def arrived(ref, sem):
+        pltpu.make_async_copy(ref, ref, sem).wait()
+
     def start_halo(src, halo, send, recv):
-        out = [remote(src, halo.at[s], send.at[s], recv.at[s], at(o)) for s, o in halo_sends]
-        for c in out:
-            c.start()
-        return out
-
-    first = start_halo(b_in, halo1, h1s, h1r)
+        for s, o in halo_sends:
+            side = 1 if s in slots[1] else 0
+            remote(src, halo.at[s], send.at[0], recv.at[side], at(o)).start()
+
+    start_halo(b_in, halo1, h1s, h1r)
 
     for c in loads:
         c.wait()
@@ -133,11 +136,10 @@
         c.start()
 
     inside = ((0,), (7, 8)) if xs == 2 else ((0,), (7,), (8,))
-    sides, slots = [(), ()], [(), ()]
+    sides = [(), ()]
     for a in range(3):
         pair = ((1 + 2 * a,), (2 + 2 * a,))
         sides[a // 2] += pair if sizes[a] > 2 else (pair[0] + pair[1],)
-        slots[a // 2] += (2 * a, 2 * a + 1) if sizes[a] > 2 else (2 * a,)
 
     for x in range(xs):
         copies[x].wait()
@@ -160,11 +162,9 @@
             out.append(multiply(x, fields, 0))
         return out
 
-    def halo_part(halo, base, sends):
+    def halo_part(halo, base, recv):
         for group in range(2):
-            for (slot, _), c in zip(halo_sends, sends):
-                if slot in slots[group]:
-                    c.wait_recv()
+            arrived(halo.at[pl.ds(slots[group][0], len(slots[group]))], recv.at[group])
             begin = len(inside) + (len(sides[0]) if group else 0)
             base = [
                 base[x] + multiply(x, [halo[i, x] for i in slots[group]], begin)
@@ -192,48 +192,45 @@
 
     def to_near(i, count):
         here = pl.ds(0, count)
-        out = [
+        for j, f in enumerate(near_sends):
             remote(
-                near.at[i, 0, here], near.at[i, j + 1, here], nrs.at[i, j], nrr.at[i, j], across(f)
-            )
-            for j, f in enumerate(near_sends)
-        ]
-        for c in out:
-            c.start()
-        return out
-
-    def to_far(i, count, arriving):
+                near.at[i, 0, here], near.at[i, j + 1, here], nrs.at[i], nrr.at[i], across(f)
+            ).start()
+
+    def near_slots(i, count):
+        return near.at[i, pl.ds(1, len(near_sends)), pl.ds(0, count)]
+
+    def far_slots(i, count):
+        return far.at[i, pl.ds(1, len(far_sends)), pl.ds(0, count)]
+
+    def to_far(i, count):
         here = pl.ds(0, count)
-        for c in arriving:
-            c.wait_recv()
+        arrived(near_slots(i, count), nrr.at[i])
         total = near[i, 0, here]
         for j in range(len(near_sends)):
             total = total + near[i, j + 1, here]
         far[i, 0, here] = total
-        out = [
-            remote(far.at[i, 0, here], far.at[i, j + 1, here], frs.at[i, j], frr.at[i, j], at(o))
-            for j, o in enumerate(far_sends)
-        ]
-        for c in out:
-            c.start()
-        return out
+        for j, o in enumerate(far_sends):
+            remote(
+                far.at[i, 0, here], far.at[i, j + 1, here], frs.at[i], frr.at[i], at(o)
+            ).start()
 
     bs = [b_ref[x] for x in range(xs)]
     base = local_part(bs)
     near[0, 0, pl.ds(0, part)] = restricted(bs)
-    w1s = halo_part(halo1, base, first)
+    w1s = halo_part(halo1, base, h1r)
     for x in range(xs):
         w1[x] = w1s[x]
-    second = start_halo(w1, halo2, h2s, h2r)
+    start_halo(w1, halo2, h2s, h2r)
 
     base = local_part(w1s)
     near[0, 0, pl.ds(part, part)] = restricted(w1s)
     near[0, 0, pl.ds(2 * part, 1)] = products((w1s, w1s), (w1s, bs))
-    near_e = to_near(0, 2 * part + 1)
-    w2s = halo_part(halo2, base, second)
+    to_near(0, 2 * part + 1)
+    w2s = halo_part(halo2, base, h2r)
     near[1, 0, pl.ds(0, part)] = restricted(w2s)
     near[1, 0, pl.ds(part, 1)] = products((w1s, w2s), (w2s, w2s), (w2s, bs))
-    near_l = to_near(1, part + 1)
+    to_near(1, part + 1)
     gather = [
         remote(mine, mine, ivs.at[i], ivr.at[i], at(o)) for i, o in enumerate(inv_sends)
     ]
@@ -241,7 +238,7 @@
         c.start()
     for x in range(xs):
         w2[x] = w2s[x]
-    far_e = to_far(0, 2 * part + 1, near_e)
+    to_far(0, 2 * part + 1)
 
     pair = 2 if groups % 2 == 0 else 1
 
@@ -270,7 +267,7 @@
         zero = jnp.zeros((2 * count * nrhs, 2 * width), F32)
         return fold(loop(groups // pair, lift_step, zero))
 
-    far_l = to_far(1, part + 1, near_l)
+    to_far(1, part + 1)
     for c in early + gather:
         c.wait_recv()
 
@@ -296,13 +293,19 @@
 
     loop(groups, prepare, 0)
 
-    for c in first + early + gather + second + near_e + near_l:
+    for c in early + gather:
         c.wait_send()
-    for c in far_e:
-        c.wait_recv()
+    every = pl.ds(0, len(halo_sends))
+    for halo, sem in ((halo1, h1s), (halo2, h2s)):
+        arrived(halo.at[every], sem.at[0])
+    rows_of = (2 * part + 1, part + 1)
+    for i in range(2):
+        arrived(near_slots(i, rows_of[i]), nrs.at[i])
+    arrived(far_slots(0, rows_of[0]), frr.at[0])
     lift_early = lift(0, 2)
-    for c in far_l:
-        c.wait_recv()
+    for i in range(2):
+        arrived(far_slots(i, rows_of[i]), frs.at[i])
+    arrived(far_slots(1, rows_of[1]), frr.at[1])
     lift_late = lift(1, 1)
 
     def add(g, acc):
@@ -337,8 +340,6 @@
             - push * lift_early[nrhs:, cols]
             + turn * lift_late[:, cols]
         )
-    for c in far_e + far_l:
-        c.wait_send()
 
 
 def finish(sol_ref, resid_ref, sol_out, resid_out, sem):
@@ -388,10 +389,10 @@
             pltpu.VMEM((2, 8, 3 * part, comps), F32),
             pltpu.VMEM((2, groups, 3 * part, comps), F32),
             dma((xs,)),
-            dma((6,)), dma((6,)), dma((6,)), dma((6,)),
+            dma((1,)), dma((2,)), dma((1,)), dma((2,)),
             dma((sizes[2],)), dma((sizes[2],)),
             dma((groups,)), dma((groups,)),
-            dma((2, 7)), dma((2, 7)), dma((2, groups)), dma((2, groups)),
+            dma((2,)), dma((2,)), dma((2,)), dma((2,)),
         ],
         compiler_params=pltpu.CompilerParams(
             collective_id=0,

time: 23 us -> 22.8 us (level)
  no operation moved by 1% of the time
where the time goes in v6:
time: 22.8 us; the launch traced here: 22.6 us
  Pallas kernels  22 us (96%)
  between operations  0.64 us (3%)
    pallas_call x1, Pallas kernels, body(): pl.pallas_call(functools.partial(kernel, sizes), out_shape=(field, field)...  21.3 us
    pallas_call x1, Pallas kernels, body(): pl.pallas_call(finish, out_shape=(field, field), in_specs=[vmem, vmem], o...  0.65 us

profile of v6, /device:TPU:0, one launch (start us, length us, event | category | flops | bytes accessed | tf_op | source)
XLA Modules:
  0.0 22.6 jit_solution(97087366466311151)
XLA Ops:
  0.6 21.3 %shard_map.68 = (f32[2,32,128]{2,1,0:T(8,128)S(1)}, f32[2,32,128]{2,1,0:T(8,128)S(1)}) custom-call(s32[2]{0:T(128)} %bitcast.11, f32[2,32,128]{2,1,0:T(8,128)} %bitcast.8, f32[2,9,128,128]{3,2,1,0:T(8,128)} %bitcast.7, f32[2,32,128]{2,1,0:T(8,128)} %bitcast.9, f32[1,32,128]{2,1,0:T(8,128)} %bitcast.10), custom_call_target="tpu_custom_call" | custom-call | tf_op jit(solution)/shard_map/pallas_call | solution.py:369
  22.0 0.6 %shard_map.69 = (f32[2,32,128]{2,1,0:T(8,128)}, f32[2,32,128]{2,1,0:T(8,128)}) custom-call(f32[2,32,128]{2,1,0:T(8,128)S(1)} %get-tuple-element.6.sol_ref, f32[2,32,128]{2,1,0:T(8,128)S(1)} %get-tuple-element.7.resid_ref), custom_call_target="tpu_custom_call" | custom-call | tf_op jit(solution)/shard_map/pallas_call | solution.py:414

commit v7 on v6

--- a/solution.py
+++ b/solution.py
@@ -162,15 +162,17 @@
             out.append(multiply(x, fields, 0))
         return out
 
-    def halo_part(halo, base, recv):
+    def halo_part(halo, base, recv, emit):
+        out = []
         for group in range(2):
             arrived(halo.at[pl.ds(slots[group][0], len(slots[group]))], recv.at[group])
             begin = len(inside) + (len(sides[0]) if group else 0)
-            base = [
-                base[x] + multiply(x, [halo[i, x] for i in slots[group]], begin)
-                for x in range(xs)
-            ]
-        return [fold(o) for o in base]
+            for x in range(xs):
+                base[x] = base[x] + multiply(x, [halo[i, x] for i in slots[group]], begin)
+                if group:
+                    out.append(fold(base[x]))
+                    emit(x, out[x])
+        return out
 
     lane = lax.broadcasted_iota(jnp.int32, (part, comps), 1)
     slot = lane // k3
@@ -218,16 +220,19 @@
     bs = [b_ref[x] for x in range(xs)]
     base = local_part(bs)
     near[0, 0, pl.ds(0, part)] = restricted(bs)
-    w1s = halo_part(halo1, base, h1r)
-    for x in range(xs):
-        w1[x] = w1s[x]
-    start_halo(w1, halo2, h2s, h2r)
-
+    def emit_first(x, image):
+        w1[x] = image
+        start_halo(w1.at[x], halo2.at[:, x], h2s, h2r)
+
+    def emit_second(x, image):
+        w2[x] = image
+
+    w1s = halo_part(halo1, base, h1r, emit_first)
     base = local_part(w1s)
     near[0, 0, pl.ds(part, part)] = restricted(w1s)
     near[0, 0, pl.ds(2 * part, 1)] = products((w1s, w1s), (w1s, bs))
     to_near(0, 2 * part + 1)
-    w2s = halo_part(halo2, base, h2r)
+    w2s = halo_part(halo2, base, h2r, emit_second)
     near[1, 0, pl.ds(0, part)] = restricted(w2s)
     near[1, 0, pl.ds(part, 1)] = products((w1s, w2s), (w2s, w2s), (w2s, bs))
     to_near(1, part + 1)
@@ -236,8 +241,6 @@
     ]
     for c in gather:
         c.start()
-    for x in range(xs):
-        w2[x] = w2s[x]
     to_far(0, 2 * part + 1)
 
     pair = 2 if groups % 2 == 0 else 1

time: 22.8 us -> 22.8 us (level)
  no operation moved by 1% of the time
where the time goes in v7:
time: 22.8 us; the launch traced here: 22.6 us
  Pallas kernels  22 us (96%)
  between operations  0.64 us (3%)
    pallas_call x1, Pallas kernels, body(): pl.pallas_call(functools.partial(kernel, sizes), out_shape=(field, field)...  21.3 us
    pallas_call x1, Pallas kernels, body(): pl.pallas_call(finish, out_shape=(field, field), in_specs=[vmem, vmem], o...  0.65 us

profile of v7, /device:TPU:0, one launch (start us, length us, event | category | flops | bytes accessed | tf_op | source)
XLA Modules:
  0.0 22.6 jit_solution(11744633774004668585)
XLA Ops:
  0.6 21.3 %shard_map.68 = (f32[2,32,128]{2,1,0:T(8,128)S(1)}, f32[2,32,128]{2,1,0:T(8,128)S(1)}) custom-call(s32[2]{0:T(128)} %bitcast.11, f32[2,32,128]{2,1,0:T(8,128)} %bitcast.8, f32[2,9,128,128]{3,2,1,0:T(8,128)} %bitcast.7, f32[2,32,128]{2,1,0:T(8,128)} %bitcast.9, f32[1,32,128]{2,1,0:T(8,128)} %bitcast.10), custom_call_target="tpu_custom_call" | custom-call | tf_op jit(solution)/shard_map/pallas_call | solution.py:372
  22.0 0.6 %shard_map.69 = (f32[2,32,128]{2,1,0:T(8,128)}, f32[2,32,128]{2,1,0:T(8,128)}) custom-call(f32[2,32,128]{2,1,0:T(8,128)S(1)} %get-tuple-element.6.sol_ref, f32[2,32,128]{2,1,0:T(8,128)S(1)} %get-tuple-element.7.resid_ref), custom_call_target="tpu_custom_call" | custom-call | tf_op jit(solution)/shard_map/pallas_call | solution.py:417

commit v8 on v6

--- a/solution.py
+++ b/solution.py
@@ -162,8 +162,10 @@
             out.append(multiply(x, fields, 0))
         return out
 
-    def halo_part(halo, base, recv):
+    def halo_part(halo, base, recv, between=lambda: None):
         for group in range(2):
+            if group:
+                between()
             arrived(halo.at[pl.ds(slots[group][0], len(slots[group]))], recv.at[group])
             begin = len(inside) + (len(sides[0]) if group else 0)
             base = [
@@ -226,8 +228,7 @@
     base = local_part(w1s)
     near[0, 0, pl.ds(part, part)] = restricted(w1s)
     near[0, 0, pl.ds(2 * part, 1)] = products((w1s, w1s), (w1s, bs))
-    to_near(0, 2 * part + 1)
-    w2s = halo_part(halo2, base, h2r)
+    w2s = halo_part(halo2, base, h2r, lambda: to_near(0, 2 * part + 1))
     near[1, 0, pl.ds(0, part)] = restricted(w2s)
     near[1, 0, pl.ds(part, 1)] = products((w1s, w2s), (w2s, w2s), (w2s, bs))
     to_near(1, part + 1)

time: 22.8 us -> 22.5 us (0.987)
  Pallas kernels: 22 us -> 21.7 us
    pallas_call x1, Pallas kernels: 21.3 us -> 21.1 us  [body(): pl.pallas_call(functools.partial(kernel, sizes), out_shape=(field, field)...]
where the time goes in v8:
time: 22.5 us; the launch traced here: 22.4 us
  Pallas kernels  21.7 us (96%)
  between operations  0.64 us (3%)
    pallas_call x1, Pallas kernels, body(): pl.pallas_call(functools.partial(kernel, sizes), out_shape=(field, field)...  21.1 us
    pallas_call x1, Pallas kernels, body(): pl.pallas_call(finish, out_shape=(field, field), in_specs=[vmem, vmem], o...  0.65 us

profile of v8, /device:TPU:0, one launch (start us, length us, event | category | flops | bytes accessed | tf_op | source)
XLA Modules:
  0.0 22.4 jit_solution(10765981310288350460)
XLA Ops:
  0.6 21.1 %shard_map.68 = (f32[2,32,128]{2,1,0:T(8,128)S(1)}, f32[2,32,128]{2,1,0:T(8,128)S(1)}) custom-call(s32[2]{0:T(128)} %bitcast.11, f32[2,32,128]{2,1,0:T(8,128)} %bitcast.8, f32[2,9,128,128]{3,2,1,0:T(8,128)} %bitcast.7, f32[2,32,128]{2,1,0:T(8,128)} %bitcast.9, f32[1,32,128]{2,1,0:T(8,128)} %bitcast.10), custom_call_target="tpu_custom_call" | custom-call | tf_op jit(solution)/shard_map/pallas_call | solution.py:370
  21.7 0.6 %shard_map.69 = (f32[2,32,128]{2,1,0:T(8,128)}, f32[2,32,128]{2,1,0:T(8,128)}) custom-call(f32[2,32,128]{2,1,0:T(8,128)S(1)} %get-tuple-element.6.sol_ref, f32[2,32,128]{2,1,0:T(8,128)S(1)} %get-tuple-element.7.resid_ref), custom_call_target="tpu_custom_call" | custom-call | tf_op jit(solution)/shard_map/pallas_call | solution.py:415
